TPU v7x, 32 devices: a whole 2x2x4 slice. The times are simulated.
32 devices in a mesh: dp: 8 (over z, x), tensor: 4 (over y, core).
Axes of the slice: x: 2, y: 2, z: 4, core: 2. Of those that a mesh axis runs over, the one named last changes fastest.
Arguments:
- inputs: bfloat16 [8192, 768], P(('dp', 'tensor')), may hold values from -6 to 6
- first_gain: bfloat16 [768], P('dp'), may hold values from 0.25 to 1.75
- qkv_weight: bfloat16 [768, 12, 192], P('dp', 'tensor'), may hold values from -0.21875 to 0.21875
- out_weight: bfloat16 [768, 768], P('tensor', 'dp'), may hold values from -0.875 to 0.875
- bias_table: bfloat16 [32, 12], P(None, 'tensor'), may hold values from -4 to 4
- second_gain: bfloat16 [768], P('dp'), may hold values from 0.25 to 1.75
- router_weight: bfloat16 [768, 8], P('dp'), may hold values from -0.15625 to 0.15625
- expert_in: bfloat16 [8, 768, 3072], P('dp', None, 'tensor'), may hold values from -0.21875 to 0.21875
- expert_output_weights: bfloat16 [8, 3072, 768], P('dp', 'tensor'), may hold values from -0.15625 to 0.15625
- segments: int32 [8, 1024], P('dp'), may hold values from 0 to 2, never falling along the last dimension, each value on 1 to 512 neighbouring positions
- buckets: int32 [1024], replicated, may hold values from 0 to 31, as said below
- choices: int32 [8192, 2], P(('dp', 'tensor')), may hold values from 0 to 7, all different within a row; in each aligned block of 256 rows (0 to 255, 256 to 511, ...) at most 128 rows name the same one
- cotangent: bfloat16 [8192, 768], P(('dp', 'tensor')), may hold values from -6 to 6
Outputs:
- result: float32 [8192, 768], P(('dp', 'tensor'))
- grad_inputs: float32 [8192, 768], P(('dp', 'tensor'))
- grad_first_gain: float32 [768], P(('dp', 'tensor'))
- grad_qkv_weight: float32 [768, 12, 192], P('dp', 'tensor')
- grad_out_weight: float32 [768, 768], P('tensor', 'dp')
- grad_bias_table: float32 [32, 12], P(None, 'tensor')
- gradient_second_norm_gain: float32 [768], P(('dp', 'tensor'))
- grad_router_weight: float32 [768, 8], P(('dp', 'tensor'))
- grad_expert_in: float32 [8, 768, 3072], P('dp', None, 'tensor')
- grad_expert_out: float32 [8, 3072, 768], P('dp', 'tensor')
Inputs may be any that keep to these rules, and one draw needn't show every extreme that they name: `choices`: within each aligned block of 256 rows (the rows of one device) no expert is named by more than 128 rows; a row names two different experts. `buckets`: never falling with the distance; 0 at distance 0 and 31 at distance 1024 - 1. `segments`: never falling along a sequence; every document has 1 to 512 positions.
All inputs are finite; a program needn't handle non-finite values.
Results may differ from a plain program's by a relative error of at most 0.02.
Values may be sent and summed in bfloat16 or wider, within the bound.
A program may use at most 192 MiB of HBM per device.

v0:
```python
import jax
import jax.numpy as jnp
from jax import lax
from jax.sharding import PartitionSpec as P

EPSILON = 1e-06
MASKED = -1e30


def rms_scale(values):
    return lax.rsqrt(jnp.mean(values * values, axis=-1, keepdims=True) + EPSILON)


def norm_backward(grad_normed, values, norm_scale, gain_vec):
    weighted = grad_normed * gain_vec
    grad_gain = jnp.sum(grad_normed * values * norm_scale, axis=0)
    grad_values = norm_scale * weighted - values * norm_scale * norm_scale * norm_scale * jnp.mean(
        weighted * values, axis=-1, keepdims=True
    )
    return (grad_values, grad_gain)


def slot_table(expert_ids, num_experts):
    flat_ids = expert_ids.reshape(-1)
    onehot = (flat_ids[:, None] == jnp.arange(num_experts, dtype=jnp.int32)[None, :]).astype(
        jnp.int32
    )
    before = jnp.cumsum(onehot, axis=0) - onehot
    return jnp.sum(before * onehot, axis=1).reshape(expert_ids.shape)


def causal_mask(length):
    position = jnp.arange(length, dtype=jnp.int32)
    return position[None, :] <= position[:, None]


def bucket_bounds(buckets, bucket_count):
    levels = jnp.arange(bucket_count + 1, dtype=jnp.int32)
    return jnp.sum((buckets[None, :] < levels[:, None]).astype(jnp.int32), axis=1)


def tile_onehot(bounds, start, tile_rows, length):
    query_pos = start + jnp.arange(tile_rows, dtype=jnp.int32)
    gap = query_pos[:, None] - jnp.arange(length, dtype=jnp.int32)[None, :]
    inside = (gap[:, :, None] >= bounds[None, None, :-1]) & (
        gap[:, :, None] < bounds[None, None, 1:]
    )
    return inside.astype(jnp.bfloat16)


def score_block(queries, key_rows, seg_ids, bias_full, head_dim):
    scores = (
        jnp.einsum("qhe,khe->hqk", queries, key_rows, preferred_element_type=jnp.float32)
        * head_dim ** (-0.5)
        + bias_full
    )
    allowed = causal_mask(seg_ids.shape[0]) & (seg_ids[:, None] == seg_ids[None, :])
    return jnp.where(allowed[None], scores, MASKED)


def attend_one(qkv_seq, seg_ids, bias_full, head_dim):
    queries = qkv_seq[..., :head_dim]
    key_rows = qkv_seq[..., head_dim : 2 * head_dim]
    value_rows = qkv_seq[..., 2 * head_dim :]
    scores = score_block(queries, key_rows, seg_ids, bias_full, head_dim)
    top_score = jnp.max(scores, axis=-1, keepdims=True)
    exponent = jnp.exp(scores - top_score)
    running = jnp.sum(exponent, axis=-1, keepdims=True)
    weights = (exponent / running).astype(jnp.bfloat16)
    mixed_out = jnp.einsum(
        "hqk,khe->qhe", weights, value_rows, preferred_element_type=jnp.float32
    ).astype(jnp.bfloat16)
    log_total = (top_score + jnp.log(running))[..., 0]
    return (mixed_out, log_total)


def attend_back(qkv_seq, seg_ids, bias_full, log_total, grad_mixed, head_dim, bounds, tile_rows):
    queries = qkv_seq[..., :head_dim]
    key_rows = qkv_seq[..., head_dim : 2 * head_dim]
    value_rows = qkv_seq[..., 2 * head_dim :]
    scores = score_block(queries, key_rows, seg_ids, bias_full, head_dim)
    weights = jnp.exp(scores - log_total[..., None])
    grad_values = jnp.einsum(
        "hqk,qhe->khe", weights.astype(jnp.bfloat16), grad_mixed, preferred_element_type=jnp.float32
    )
    grad_weights = jnp.einsum(
        "qhe,khe->hqk", grad_mixed, value_rows, preferred_element_type=jnp.float32
    )
    row_delta = jnp.sum(weights * grad_weights, axis=-1, keepdims=True)
    grad_scores = (weights * (grad_weights - row_delta)).astype(jnp.bfloat16)
    factor = head_dim ** (-0.5)
    grad_queries = (
        jnp.einsum("hqk,khe->qhe", grad_scores, key_rows, preferred_element_type=jnp.float32)
        * factor
    )
    grad_keys = (
        jnp.einsum("hqk,qhe->khe", grad_scores, queries, preferred_element_type=jnp.float32)
        * factor
    )
    gradient_query_key_value = jnp.concatenate(
        [grad_queries, grad_keys, grad_values], axis=-1
    ).astype(jnp.bfloat16)
    heads_here, length, _ = grad_scores.shape
    tile_count = length // tile_rows
    tiled = grad_scores.reshape(heads_here, tile_count, tile_rows, length)

    def add_tile(total, tile_idx):
        piece = lax.dynamic_index_in_dim(tiled, tile_idx, 1, keepdims=False)
        onehot = tile_onehot(bounds, tile_idx * tile_rows, tile_rows, length)
        return (
            total + jnp.einsum("hqk,qkb->hb", piece, onehot, preferred_element_type=jnp.float32),
            None,
        )

    start_total = jnp.zeros((heads_here, bounds.shape[0] - 1), jnp.float32)
    table_part, _ = lax.scan(add_tile, start_total, jnp.arange(tile_count, dtype=jnp.int32))
    return (gradient_query_key_value, table_part)


def to_experts(buffer):
    joined = lax.all_gather(buffer, "tensor", axis=1, tiled=True)
    return lax.all_to_all(joined, "dp", split_axis=0, concat_axis=0, tiled=True)


def from_experts(partial_rows):
    returned = lax.all_to_all(partial_rows, "dp", split_axis=0, concat_axis=0, tiled=True)
    return lax.psum_scatter(
        returned.astype(jnp.float32).astype(jnp.bfloat16), "tensor", scatter_dimension=1, tiled=True
    ).astype(jnp.float32)


def body(
    inputs,
    first_gain,
    qkv_weight,
    out_weight,
    bias_table,
    second_gain,
    router_weight,
    expert_in,
    expert_output_weights,
    segments,
    buckets,
    choices,
    cotangent,
):
    query_key_value_complete, out_full, first_full, second_full, router_full = (
        lax.all_gather(qkv_weight, "dp", axis=0, tiled=True),
        lax.all_gather(out_weight, "dp", axis=1, tiled=True),
        lax.all_gather(first_gain, "dp", axis=0, tiled=True),
        lax.all_gather(second_gain, "dp", axis=0, tiled=True),
        lax.all_gather(router_weight, "dp", axis=0, tiled=True),
    )
    tokens_dev, model_width = inputs.shape
    wide_size = lax.axis_size("dp")
    experts = router_full.shape[1]
    top_count = choices.shape[1]
    capacity = max(2, 2 * top_count * tokens_dev // experts)
    heads_dev = query_key_value_complete.shape[1]
    head_dim = query_key_value_complete.shape[2] // 3
    seq_count, seq_len = segments.shape
    bucket_count = bias_table.shape[0]
    bounds = bucket_bounds(buckets, bucket_count)
    tile_rows = min(128, seq_len)
    tile_count = seq_len // tile_rows

    def bias_tile(tile_idx):
        onehot = tile_onehot(bounds, tile_idx * tile_rows, tile_rows, seq_len)
        return jnp.einsum("qkb,bh->hqk", onehot, bias_table, preferred_element_type=jnp.float32)

    bias_tiles = lax.map(bias_tile, jnp.arange(tile_count, dtype=jnp.int32))
    bias_full = jnp.transpose(bias_tiles, (1, 0, 2, 3)).reshape(heads_dev, seq_len, seq_len)
    input_f = inputs.astype(jnp.float32)
    first_scale = rms_scale(input_f)
    first_f = first_full.astype(jnp.float32)
    normed_one = (input_f * first_scale * first_f).astype(jnp.bfloat16)
    group_rows = lax.all_gather(normed_one, "tensor", axis=0, tiled=True)
    sequence_token_rows = group_rows.reshape(seq_count, seq_len, model_width)
    qkv_all = jnp.einsum(
        "cvt,tqx->cvqx",
        sequence_token_rows,
        query_key_value_complete,
        preferred_element_type=jnp.float32,
    ).astype(jnp.bfloat16)

    def forward_one(packed):
        return attend_one(packed[0], packed[1], bias_full, head_dim)

    mixed_all, log_totals = lax.map(forward_one, (qkv_all, segments))
    mixed_flat = mixed_all.reshape(seq_count * seq_len, heads_dev * head_dim)
    partial_attn = jnp.dot(mixed_flat, out_full, preferred_element_type=jnp.float32)
    attn_piece = lax.psum_scatter(
        partial_attn.astype(jnp.bfloat16), "tensor", scatter_dimension=0, tiled=True
    ).astype(jnp.float32)
    hidden = input_f + attn_piece
    second_scale = rms_scale(hidden)
    second_f = second_full.astype(jnp.float32)
    normed_two = (hidden * second_scale * second_f).astype(jnp.bfloat16)
    logits = jnp.dot(normed_two, router_full, preferred_element_type=jnp.float32)
    router_probs = jax.nn.softmax(logits, axis=-1)
    picked = jnp.take_along_axis(router_probs, choices, axis=1)
    selected_gate_sum = jnp.sum(picked, axis=1, keepdims=True)
    gate_values = picked / selected_gate_sum
    slot_ids = slot_table(choices, experts)
    target = (choices * capacity + slot_ids).reshape(-1)
    pair_count = tokens_dev * top_count
    source = (
        jnp.full((experts * capacity,), pair_count, jnp.int32)
        .at[target]
        .set(jnp.arange(pair_count, dtype=jnp.int32))
    )
    token_of_slot = source // top_count
    padded_two = jnp.concatenate([normed_two, jnp.zeros((1, model_width), jnp.bfloat16)], axis=0)
    send_rows = padded_two[token_of_slot].reshape(experts, capacity, model_width)
    recv_rows = to_experts(send_rows)
    local_experts = expert_in.shape[0]
    rows_four = recv_rows.reshape(wide_size, local_experts, -1, model_width)
    upward = jnp.einsum("sxrd,xdf->sxrf", rows_four, expert_in, preferred_element_type=jnp.float32)
    active = jax.nn.gelu(upward).astype(jnp.bfloat16)
    out_part = jnp.einsum(
        "sxrf,xfd->sxrd", active, expert_output_weights, preferred_element_type=jnp.float32
    ).astype(jnp.bfloat16)
    expert_result = from_experts(out_part.reshape(experts, -1, model_width))
    per_choice = expert_result.reshape(experts * capacity, model_width)[target].reshape(
        tokens_dev, top_count, model_width
    )
    result = hidden + jnp.sum(gate_values[..., None] * per_choice, axis=1)
    grad_out = cotangent.astype(jnp.float32)
    grad_pairs = gate_values[..., None] * grad_out[:, None, :]
    padded_grad = jnp.concatenate(
        [grad_pairs.reshape(pair_count, model_width), jnp.zeros((1, model_width), jnp.float32)],
        axis=0,
    )
    grad_send = padded_grad[source].astype(jnp.bfloat16).reshape(experts, capacity, model_width)
    grad_gate = jnp.sum(per_choice * grad_out[:, None, :], axis=-1)
    grad_picked = (
        grad_gate - jnp.sum(gate_values * grad_gate, axis=1, keepdims=True)
    ) / selected_gate_sum
    expert_range = jnp.arange(experts, dtype=jnp.int32)
    grad_probs = jnp.sum(
        jnp.where(choices[:, :, None] == expert_range[None, None, :], grad_picked[:, :, None], 0.0),
        axis=1,
    )
    grad_logits = (
        router_probs * (grad_probs - jnp.sum(router_probs * grad_probs, axis=1, keepdims=True))
    ).astype(jnp.bfloat16)
    grad_router = jnp.einsum(
        "td,te->de", normed_two, grad_logits, preferred_element_type=jnp.float32
    )
    grad_normed = jnp.einsum(
        "te,de->td", grad_logits, router_full, preferred_element_type=jnp.float32
    )
    grad_rows = to_experts(grad_send)
    grad_four = grad_rows.reshape(wide_size, local_experts, -1, model_width)
    grad_active = jnp.einsum(
        "sxrd,xfd->sxrf", grad_four, expert_output_weights, preferred_element_type=jnp.float32
    )
    grad_expert_out = jnp.einsum(
        "sxrf,sxrd->xfd", active, grad_four, preferred_element_type=jnp.float32
    )
    grad_upward = jax.vjp(jax.nn.gelu, upward)[1](grad_active)[0].astype(jnp.bfloat16)
    grad_expert_in = jnp.einsum(
        "sxrd,sxrf->xdf", rows_four, grad_upward, preferred_element_type=jnp.float32
    )
    grad_part = jnp.einsum(
        "sxrf,xdf->sxrd", grad_upward, expert_in, preferred_element_type=jnp.float32
    ).astype(jnp.bfloat16)
    grad_slots = from_experts(grad_part.reshape(experts, -1, model_width))
    grad_normed = grad_normed + jnp.sum(
        grad_slots.reshape(experts * capacity, model_width)[target].reshape(
            tokens_dev, top_count, model_width
        ),
        axis=1,
    )
    grad_hidden_norm, grad_second = norm_backward(grad_normed, hidden, second_scale, second_f)
    grad_hidden = grad_out + grad_hidden_norm
    grad_group = lax.all_gather(grad_hidden.astype(jnp.bfloat16), "tensor", axis=0, tiled=True)
    grad_out_weight = jnp.einsum(
        "tm,td->md", mixed_flat, grad_group, preferred_element_type=jnp.float32
    )
    grad_mixed = jnp.einsum(
        "td,md->tm", grad_group, out_full, preferred_element_type=jnp.float32
    ).astype(jnp.bfloat16)
    grad_mixed = grad_mixed.reshape(seq_count, seq_len, heads_dev, head_dim)

    def backward_one(packed):
        return attend_back(
            packed[0], packed[1], bias_full, packed[2], packed[3], head_dim, bounds, tile_rows
        )

    gradient_query_key_value, table_parts = lax.map(
        backward_one, (qkv_all, segments, log_totals, grad_mixed)
    )
    grad_qkv_weight = jnp.einsum(
        "bck,bcwz->kwz",
        sequence_token_rows,
        gradient_query_key_value,
        preferred_element_type=jnp.float32,
    )
    grad_normed_one = jnp.einsum(
        "igaq,uaq->igu",
        gradient_query_key_value,
        query_key_value_complete,
        preferred_element_type=jnp.float32,
    ).reshape(-1, model_width)
    grad_first_in = lax.psum_scatter(
        grad_normed_one.astype(jnp.bfloat16), "tensor", scatter_dimension=0, tiled=True
    ).astype(jnp.float32)
    grad_inputs_norm, grad_first = norm_backward(grad_first_in, input_f, first_scale, first_f)
    grad_inputs = grad_hidden + grad_inputs_norm
    table_grad = jnp.transpose(jnp.sum(table_parts, axis=0), (1, 0))
    grad_table = lax.psum(table_grad, "dp")
    grad_qkv_shard, grad_out_shard = (
        lax.psum_scatter(grad_qkv_weight, "dp", scatter_dimension=0, tiled=True),
        lax.psum_scatter(grad_out_weight, "dp", scatter_dimension=1, tiled=True),
    )
    grad_first_shard, grad_second_shard, grad_router_shard = (
        lax.psum_scatter(grad_first, ("dp", "tensor"), scatter_dimension=0, tiled=True),
        lax.psum_scatter(grad_second, ("dp", "tensor"), scatter_dimension=0, tiled=True),
        lax.psum_scatter(grad_router, ("dp", "tensor"), scatter_dimension=0, tiled=True),
    )
    return (
        result,
        grad_inputs,
        grad_first_shard,
        grad_qkv_shard,
        grad_out_shard,
        grad_table,
        grad_second_shard,
        grad_router_shard,
        grad_expert_in,
        grad_expert_out,
    )


def solution(mesh):
    return jax.shard_map(
        body,
        mesh=mesh,
        in_specs=(
            P(("dp", "tensor"), None),
            P("dp"),
            P("dp", "tensor", None),
            P("tensor", "dp"),
            P(None, "tensor"),
            P("dp"),
            P("dp", None),
            P("dp", None, "tensor"),
            P("dp", "tensor", None),
            P("dp", None),
            P(),
            P(("dp", "tensor"), None),
            P(("dp", "tensor"), None),
        ),
        out_specs=(
            P(("dp", "tensor"), None),
            P(("dp", "tensor"), None),
            P(("dp", "tensor")),
            P("dp", "tensor", None),
            P("tensor", "dp"),
            P(None, "tensor"),
            P(("dp", "tensor")),
            P(("dp", "tensor"), None),
            P("dp", None, "tensor"),
            P("dp", "tensor", None),
        ),
        check_vma=False,
    )
```

profile of v0, /device:TPU:0, one launch (start us, length us, event | category | flops | bytes accessed | tf_op | source)
XLA Modules:
  0.0 1286.7 jit_solution(12039995248272761865)
XLA Ops:
  10.9 23.1 %all-reduce.8 = (bf16[768]{0:T(1024)(128)(2,1)S(1)}, bf16[768]{0:T(1024)(128)(2,1)S(1)}) all-reduce(bf16[768]{0:T(1024)(128)(2,1)S(1)} %dynamic-update-slice, bf16[768]{0:T(1024)(128)(2,1)S(1)} %dynamic-update-slice.1), channel_id=1, replica_groups=mesh['dp'=8,'tensor'=4] {'dp'}, use_global_device_ids=true, to_apply=%add.2 | all-reduce | flops 1536 | bytes 6144
  38.6 57.2 %while.20 = (s32[]{:T(128)}, f32[8,3,128,1024]{3,1,2,0:T(4,128)}, s32[8]{0:T(128)S(1)}, s32[33]{0:T(128)S(1)}, bf16[32,3]{0,1:T(4,128)(2,1)}, /*index=5*/s32[]{:T(128)}, s32[1]{0:T(128)}) while((s32[]{:T(128)}, f32[8,3,128,1024]{3,1,2,0:T(4,128)}, s32[8]{0:T(128)S(1)}, s32[33]{0:T(128)S(1)}, bf16[32,3]{0,1:T(4,128)(2,1)}, ...), condition=%wide.region_3.4_spmd, body=%wide.region_2.3_spmd.sunk | while | flops 37879936 | bytes 3149161 | solution.py:171
  40.0 5.7 bitcast_dynamic-update-slice_fusion.2
  47.2 5.7 bitcast_dynamic-update-slice_fusion.2
  54.3 5.7 bitcast_dynamic-update-slice_fusion.2
  61.4 5.7 bitcast_dynamic-update-slice_fusion.2
  68.6 5.8 bitcast_dynamic-update-slice_fusion.2
  75.8 5.7 bitcast_dynamic-update-slice_fusion.2
  82.9 5.7 bitcast_dynamic-update-slice_fusion.2
  90.1 5.7 bitcast_dynamic-update-slice_fusion.2
  96.4 35.7 %all_gather.29 = bf16[768,3,192]{2,1,0:T(4,128)(2,1)S(1)} all-gather(bf16[96,3,192]{2,1,0:T(4,128)(2,1)S(1)} %copy.91), channel_id=1, replica_groups=mesh['dp'=8,'tensor'=4] {'dp'}, dimensions={0}, use_global_device_ids=true | all-gather | bytes 995328 | tf_op jit(solution)/shard_map/all_gather | solution.py:148
  134.3 17.7 %copy.93 = f32[3,8,128,1024]{3,2,1,0:T(8,128)} copy(f32[3,8,128,1024]{3,0,2,1:T(4,128)} %bitcast.185) | data formatting | bytes 25165824 | tf_op jit(solution)/shard_map/transpose | solution.py:172
  152.0 31.1 %all_gather.30 = bf16[192,768]{0,1:T(8,128)(2,1)S(1)} all-gather(bf16[192,96]{0,1:T(8,128)(2,1)S(1)} %copy.94), channel_id=1, replica_groups=mesh['dp'=8,'tensor'=4] {'dp'}, dimensions={1}, use_global_device_ids=true | all-gather | bytes 331776 | tf_op jit(solution)/shard_map/all_gather | solution.py:149
  183.8 2.5 fusion.118
  186.5 6.8 fusion.116
  193.3 2.9 fusion.24
  197.9 3.2 fusion.60
  205.5 2.4 scatter_custom_fusion
  208.6 22.5 %reduce-scatter.10.cloned.1.call-done = bf16[256,768]{1,0:T(8,128)(2,1)} async-done(((bf16[1024,768]{1,0:T(8,128)(2,1)}), bf16[256,768]{1,0:T(8,128)(2,1)}) %reduce-scatter.10.cloned.1.call-update) | async-done | bytes 393232 | tf_op jit(solution)/shard_map/reduce_scatter | solution.py:192
  234.1 5.2 gather_fusion
  239.3 46.5 %all-gather.8.cloned.1.call-done = bf16[8,512,768]{2,1,0:T(8,128)(2,1)} async-done(((bf16[8,128,768]{2,1,0:T(8,128)(2,1)}), bf16[8,512,768]{2,1,0:T(8,128)(2,1)}) %all-gather.8.cloned.1.call-update) | async-done | bytes 6291472 | tf_op jit(solution)/shard_map/all_gather | solution.py:121
  285.9 144.3 %all_to_all.20 = bf16[8,512,768]{2,1,0:T(8,128)(2,1)S(1)} all-to-all(bf16[8,512,768]{2,1,0:T(8,128)(2,1)} %all-gather.8.cloned.1.call-done), channel_id=1, replica_groups=mesh['dp'=8,'tensor'=4] {'dp'}, dimensions={0} | all-to-all | bytes 12582912 | tf_op jit(solution)/shard_map/all_to_all | solution.py:122
  430.2 2.6 copy-done.10
  432.9 5.2 fusion.69
  438.1 4.5 copy-done.62
  442.6 9.5 fusion.39
  452.1 4.9 all-to-all-start.1
  457.1 155.7 %all-gather = bf16[8,96,8]{1,2,0:T(8,128)(2,1)S(1)} all-gather(bf16[1,96,8]{1,2,0:T(8,128)(2,1)S(1)} %bitcast.198), channel_id=1, replica_groups=mesh['dp'=8,'tensor'=4] {'dp'}, dimensions={0}, use_global_device_ids=true | all-gather | bytes 13824 | tf_op jit(solution)/shard_map/all_gather | solution.py:152
  621.0 3.5 gather_fusion.4
  627.4 5.5 gather_fusion.2
  632.8 42.9 %all-gather.10.cloned.1.call-done = bf16[8,512,768]{2,1,0:T(8,128)(2,1)} async-done(((bf16[8,128,768]{2,1,0:T(8,128)(2,1)}), bf16[8,512,768]{2,1,0:T(8,128)(2,1)}) %all-gather.10.cloned.1.call-update) | async-done | bytes 6291472 | tf_op jit(solution)/shard_map/all_gather | solution.py:121
  675.7 5.5 all-to-all-start.2
  681.9 138.0 %all-to-all-done.2 = bf16[8,512,768]{2,1,0:T(8,128)(2,1)} async-done(((bf16[8,512,768]{2,1,0:T(8,128)(2,1)}), bf16[8,512,768]{2,1,0:T(8,128)(2,1)}, u32[]{:S(2)}, u32[]{:S(2)}) %all-to-all-start.2) | async-done | bytes 6291488 | tf_op jit(solution)/shard_map/all_to_all | solution.py:122
  819.9 15.3 %fusion.18 = bf16[8,1,512,768]{3,2,0,1:T(8,128)(2,1)S(1)} fusion(f32[8,512,768]{2,1,0:T(8,128)} %copy-done.62, bf16[8,512,768]{2,1,0:T(8,128)(2,1)} %all-to-all-done.2, bf16[1,768,768]{2,1,0:T(8,128)(2,1)S(1)} %copy-done), kind=kOutput, calls=%fused_computation.34 | convolution fusion | flops 4894752768 | bytes 26345472 | tf_op jit(solution)/shard_map/sxrd,xfd->sxrf/dot_general | solution.py:255
  835.2 5.4 fusion.42
  840.7 141.8 %all_to_all.21 = bf16[8,512,768]{2,1,0:T(8,128)(2,1)} all-to-all(bf16[8,512,768]{2,1,0:T(8,128)(2,1)S(1)} %fusion.42), channel_id=1, replica_groups=mesh['dp'=8,'tensor'=4] {'dp'}, dimensions={0} | all-to-all | bytes 12582912 | tf_op jit(solution)/shard_map/all_to_all | solution.py:126
  983.1 3.4 bitcast_convert_fusion.2
  986.6 5.4 gather_fusion.1
  994.3 3.9 multiply_reduce_fusion.1
  998.7 40.4 %reduce-scatter.14.cloned.1.call-done = bf16[8,128,768]{2,1,0:T(8,128)(2,1)} async-done(((bf16[8,512,768]{2,1,0:T(8,128)(2,1)}), bf16[8,128,768]{2,1,0:T(8,128)(2,1)}) %reduce-scatter.14.cloned.1.call-update) | async-done | bytes 1572880 | tf_op jit(solution)/shard_map/reduce_scatter | solution.py:127
  1039.1 3.3 bitcast_convert_fusion.1
  1042.5 5.1 gather_fusion.3
  1047.7 3.1 reshape.407
  1050.7 4.3 reduce_sum.180
  1058.8 19.7 %all-gather.12.cloned.1.call-done = bf16[1024,768]{1,0:T(8,128)(2,1)} async-done(((bf16[256,768]{1,0:T(8,128)(2,1)}), bf16[1024,768]{1,0:T(8,128)(2,1)}) %all-gather.12.cloned.1.call-update) | async-done | bytes 1572880 | tf_op jit(solution)/shard_map/all_gather | solution.py:277
  1078.5 3.1 convolution_bitcast_fusion
  1084.0 10.7 multiply_reduce_fusion
  1096.6 6.3 multiply_convert_fusion
  1108.4 2.6 bitcast_convert_fusion
  1111.3 10.1 fusion.45
  1121.5 11.5 fusion.48
  1133.2 2.9 fusion.53
  1136.2 75.9 %while.21 = (s32[]{:T(128)}, f32[3,32]{1,0:T(4,128)S(1)}, s32[8]{0:T(128)S(1)}, bf16[3,8,128,1024]{3,2,1,0:T(8,128)(2,1)}, s32[33]{0:T(128)S(1)}, /*index=5*/s32[]{:T(128)}, s32[]{:T(128)}, s32[]{:T(128)}, s32[]{:T(128)}) while((s32[]{:T(128)}, f32[3,32]{1,0:T(4,128)S(1)}, s32[8]{0:T(128)S(1)}, ...), condition=%wide.region_32.33_spmd.clone, body=%wide.region_31.32_spmd.clone.sunk | while | flops 37880136 | bytes 4983465 | solution.py:116
  1141.4 4.2 fusion.152
  1150.9 4.2 fusion.152
  1160.4 4.2 fusion.152
  1169.8 4.2 fusion.152
  1179.3 4.2 fusion.152
  1188.8 4.2 fusion.152
  1198.3 4.2 fusion.152
  1207.8 4.2 fusion.152
  1212.0 22.1 %psum.7 = f32[32,3]{0,1:T(4,128)} all-reduce(f32[32,3]{0,1:T(4,128)S(1)} %bitcast.199), channel_id=1, replica_groups=mesh['dp'=8,'tensor'=4] {'dp'}, use_global_device_ids=true, to_apply=%region_33.34 | all-reduce | flops 96 | bytes 768 | tf_op jit(solution)/shard_map/psum | solution.py:312
  1237.0 37.2 %all-reduce.7 = (f32[768]{0:T(1024)S(1)}, f32[768]{0:T(1024)S(1)}, f32[768,8]{0,1:T(8,128)S(1)}) all-reduce(f32[768]{0:T(1024)S(1)} %get-tuple-element.158, f32[768]{0:T(1024)S(1)} %get-tuple-element.154, f32[768,8]{0,1:T(8,128)S(1)} %fusion.119), channel_id=6, replica_groups=mesh['dp'=8,'tensor'=4] {'dp','tensor'}, use_global_device_ids=true, to_apply=%region_28.29.clone | all-reduce | flops 7680 | bytes 61440
  1276.1 3.3 fusion.78
  (321 shorter events, 81.6 us)
Async XLA Ops:
  7.2 435.4 %copy-start = (bf16[1,768,768]{2,1,0:T(8,128)(2,1)S(1)}, bf16[1,768,768]{2,1,0:T(8,128)(2,1)}, u32[]{:S(2)}) copy-start(bf16[1,768,768]{2,1,0:T(8,128)(2,1)} %param.25) | copy-start | bytes 3538948
  7.2 176.6 %all-gather.6.cloned.1.call-start = ((), (), s32[]{:S(2)}) async-start(), calls=%async_computation.10 | async-start | bytes 1966080 | tf_op jit(solution)/shard_map/all_gather | solution.py:177
  37.7 193.4 %reduce-scatter.10.cloned.1.call-start = ((), (), s32[]{:S(2)}) async-start(), calls=%async_computation.11 | async-start | bytes 1966080 | tf_op jit(solution)/shard_map/reduce_scatter | solution.py:192
  38.6 57.7 %copy-start.31 = (bf16[96,3,192]{2,0,1:T(8,128)(2,1)S(1)}, bf16[96,3,192]{2,0,1:T(8,128)(2,1)}, u32[]{:S(2)}) copy-start(bf16[96,3,192]{2,0,1:T(8,128)(2,1)} %param.19) | copy-start | bytes 331780
  134.3 17.7 %copy-start.41 = (bf16[192,96]{1,0:T(8,128)(2,1)S(1)}, bf16[192,96]{1,0:T(8,128)(2,1)}, u32[]{:S(2)}) copy-start(bf16[192,96]{1,0:T(8,128)(2,1)} %param.20) | copy-start | bytes 110596
  134.3 48.9 %copy-start.48 = (s32[1,1024]{1,0:T(1,128)S(1)}, s32[1,1024]{1,0:T(1,128)}, u32[]{:S(2)}) copy-start(s32[1,1024]{1,0:T(1,128)} %param.26) | copy-start | bytes 12292
  134.3 49.5 %copy-start.22 = (bf16[768,3,192]{0,2,1:T(8,128)(2,1)S(1)}, bf16[768,3,192]{0,2,1:T(8,128)(2,1)}, u32[]{:S(2)}) copy-start(bf16[768,3,192]{0,2,1:T(8,128)(2,1)} %copy.92) | copy-start | bytes 2654212
  183.2 17.9 %copy-start.14 = (bf16[192,768]{0,1:T(8,128)(2,1)}, bf16[192,768]{0,1:T(8,128)(2,1)S(1)}, u32[]{:S(2)}) copy-start(bf16[192,768]{0,1:T(8,128)(2,1)S(1)} %all_gather.30) | copy-start | bytes 884740
  186.5 9.7 copy-start.7
  193.3 4.5 copy-start.2
  193.3 4.5 copy-start.32
  197.9 3.2 copy-start.37
  197.9 5.1 copy-start.42
  197.9 33.2 %copy-start.4 = (bf16[256,768]{1,0:T(8,128)(2,1)S(1)}, bf16[256,768]{1,0:T(8,128)(2,1)}, u32[]{:S(2)}) copy-start(bf16[256,768]{1,0:T(8,128)(2,1)} %param.17) | copy-start | bytes 1179652
  202.9 83.0 %all-gather.8.cloned.1.call-start = ((), (), s32[]{:S(2)}) async-start(), calls=%async_computation.12 | async-start | bytes 7864320 | tf_op jit(solution)/shard_map/all_gather | solution.py:121
  203.1 410.7 %copy-start.16 = (s32[256,2]{1,0:T(8,128)}, s32[256,2]{1,0:T(8,128)S(1)}, u32[]{:S(2)}) copy-start(s32[256,2]{1,0:T(8,128)S(1)} %copy.99) | copy-start | bytes 6148
  203.4 28.9 %copy-start.35 = (f32[768]{0:T(1024)}, f32[768]{0:T(1024)S(1)}, u32[]{:S(2)}) copy-start(f32[768]{0:T(1024)S(1)} %convert_element_type.120) | copy-start | bytes 9220
  205.5 26.8 %copy-start.55 = (s32[512,1]{0,1:T(1,128)}, s32[512,1]{0,1:T(1,128)S(1)}, u32[]{:S(2)}) copy-start(s32[512,1]{0,1:T(1,128)S(1)} %compare_select_fusion) | copy-start | bytes 6148
  234.1 384.8 %copy-start.11 = (bf16[256,768]{1,0:T(8,128)(2,1)}, bf16[256,768]{1,0:T(8,128)(2,1)S(1)}, u32[]{:S(2)}) copy-start(bf16[256,768]{1,0:T(8,128)(2,1)S(1)} %multiply_convert_fusion.1) | copy-start | bytes 1179652
  285.9 147.0 %copy-start.59 = (bf16[1,768,768]{2,1,0:T(8,128)(2,1)S(1)}, bf16[1,768,768]{2,1,0:T(8,128)(2,1)}, u32[]{:S(2)}) copy-start(bf16[1,768,768]{2,1,0:T(8,128)(2,1)} %param.24) | copy-start | bytes 3538948
  430.2 2.6 copy-start.10
  438.1 4.5 copy-start.62
  452.1 5.0 copy-start.57
  452.1 162.8 %copy-start.13 = (bf16[256,768]{1,0:T(8,128)(2,1)S(1)}, bf16[256,768]{1,0:T(8,128)(2,1)}, u32[]{:S(2)}) copy-start(bf16[256,768]{1,0:T(8,128)(2,1)} %param.29) | copy-start | bytes 1179652
  452.1 223.6 %all-to-all-start.1 = ((bf16[8,512,768]{2,1,0:T(8,128)(2,1)}), bf16[8,512,768]{2,1,0:T(8,128)(2,1)}, u32[]{:S(2)}, u32[]{:S(2)}) async-start(bf16[8,512,768]{2,1,0:T(8,128)(2,1)} %fusion.39), calls=%async_computation.2 | async-start | bytes 12582912 | tf_op jit(solution)/shard_map/all_to_all | solution.py:126
  457.1 218.6 %all-gather.10.cloned.1.call-start = ((), (), s32[]{:S(2)}) async-start(), calls=%async_computation.14 | async-start | bytes 7864320 | tf_op jit(solution)/shard_map/all_gather | solution.py:121
  621.0 4.3 copy-start.17
  621.0 4.3 copy-start.21
  675.7 144.2 %all-to-all-start.2 = ((bf16[8,512,768]{2,1,0:T(8,128)(2,1)}), bf16[8,512,768]{2,1,0:T(8,128)(2,1)}, u32[]{:S(2)}, u32[]{:S(2)}) async-start(bf16[8,512,768]{2,1,0:T(8,128)(2,1)} %all-gather.10.cloned.1.call-done), calls=%async_computation.4 | async-start | bytes 12582912 | tf_op jit(solution)/shard_map/all_to_all | solution.py:122
  681.2 301.9 %reduce-scatter.12.cloned.1.call-start = ((), (), s32[]{:S(2)}) async-start(), calls=%async_computation.13 | async-start | bytes 7864320 | tf_op jit(solution)/shard_map/reduce_scatter | solution.py:127
  681.8 153.4 %copy-start.60 = (bf16[1,768,768]{2,1,0:T(8,128)(2,1)S(1)}, bf16[1,768,768]{2,1,0:T(8,128)(2,1)}, u32[]{:S(2)}) copy-start(bf16[1,768,768]{2,1,0:T(8,128)(2,1)} %param.24) | copy-start | bytes 3538948
  681.8 357.3 %reduce-scatter.14.cloned.1.call-start = ((), (), s32[]{:S(2)}) async-start(), calls=%async_computation.15 | async-start | bytes 7864320 | tf_op jit(solution)/shard_map/reduce_scatter | solution.py:127
  835.2 5.5 copy-start.61
  982.5 96.0 %all-gather.12.cloned.1.call-start = ((), (), s32[]{:S(2)}) async-start(), calls=%async_computation.16 | async-start | bytes 1966080 | tf_op jit(solution)/shard_map/all_gather | solution.py:277
  992.0 6.2 copy-start.50
  992.0 6.6 copy-start.43
  992.0 6.7 copy-start.30
  992.0 6.7 copy-start.45
  992.0 6.7 copy-start.52
  1042.5 12.5 copy-start.5
  1042.5 12.5 copy-start.6
  1042.5 12.5 copy-start.34
  1042.5 12.5 copy-start.36
  1042.5 12.5 copy-start.47
  1047.6 11.1 copy-start.33
  1047.7 11.1 copy-start.38
  1047.7 30.8 %copy-start.19 = (bf16[3,64,1024]{2,1,0:T(8,128)(2,1)S(1)}, bf16[3,64,1024]{2,1,0:T(8,128)(2,1)}, u32[]{:S(2)}) copy-start(bf16[3,64,1024]{2,1,0:T(8,128)(2,1)} %copy-done.18) | copy-start | bytes 1179652
  1050.7 31.1 %copy-start.15 = (bf16[192,768]{0,1:T(8,128)(2,1)S(1)}, bf16[192,768]{0,1:T(8,128)(2,1)}, u32[]{:S(2)}) copy-start(bf16[192,768]{0,1:T(8,128)(2,1)} %copy-done.14) | copy-start | bytes 884740
  1050.7 33.2 %copy-start.8 = (bf16[1024,3,192]{0,2,1:T(8,128)(2,1)S(1)}, bf16[1024,3,192]{0,2,1:T(8,128)(2,1)}, u32[]{:S(2)}) copy-start(bf16[1024,3,192]{0,2,1:T(8,128)(2,1)} %copy-done.7) | copy-start | bytes 3538948
  1058.7 175.4 %reduce-scatter.20.cloned.1.call-start = ((), (), s32[]{:S(2)}) async-start(), calls=%async_computation.19 | async-start | bytes 884736
  1081.6 154.2 %reduce-scatter.16.cloned.1.call-start = ((), (), s32[]{:S(2)}) async-start(), calls=%async_computation.17 | async-start | bytes 1966080 | tf_op jit(solution)/shard_map/reduce_scatter | solution.py:306
  1083.9 10.7 slice-start
  1083.9 10.8 slice-start.1
  1084.0 12.7 slice-start.2
  1102.9 3.3 copy-start.3
  1106.2 2.2 copy-start.24
  1111.0 168.3 %reduce-scatter.18.cloned.1.call-start = ((), (), s32[]{:S(2)}) async-start(), calls=%async_computation.18 | async-start | bytes 2654208 | tf_op jit(solution)/shard_map/reduce_scatter | solution.py:314
  1121.4 11.5 copy-start.12
  1121.4 11.7 copy-start.25
  1121.5 11.7 copy-start.58
  1133.0 3.1 copy-start.28
  1136.1 99.6 %copy-start.40 = (f32[768]{0:T(1024)S(1)}, f32[768]{0:T(1024)}, u32[]{:S(2)}) copy-start(f32[768]{0:T(1024)} %copy-done.39) | copy-start | bytes 9220
  1136.1 99.6 %copy-start.54 = (f32[256]{0:T(256)S(1)}, f32[256]{0:T(256)}, u32[]{:S(2)}) copy-start(f32[256]{0:T(256)} %copy-done.53) | copy-start | bytes 3076
  1212.0 67.4 %copy-start.1 = (bf16[1,768,768]{2,1,0:T(8,128)(2,1)S(1)}, bf16[1,768,768]{2,1,0:T(8,128)(2,1)}, u32[]{:S(2)}) copy-start(bf16[1,768,768]{2,1,0:T(8,128)(2,1)} %param.25) | copy-start | bytes 3538948
  (14 other events, 11.9 us)
Sparse Core Ops, SparseCore 0:
  37.8 17.0 all-gather.5
  203.0 28.0 reduce-scatter.9
  239.5 46.3 all-gather.7
  633.0 42.6 all-gather.9
  684.4 58.8 reduce-scatter.11
  982.6 56.4 reduce-scatter.13
  1058.8 19.6 all-gather.11
  1082.1 62.4 reduce-scatter.19
  1147.2 27.1 reduce-scatter.15
  1178.7 68.9 reduce-scatter.17
where the time goes:
time: 1290 us
  blocking collectives  591 us (46%)
  waiting for transfers between devices  311 us (24%)
  matrix products  181 us (14%)
  local copies, waits for them, and re-layouts  109 us (8%)
  other arithmetic  41.6 us (3%)
  loops' own time  26.3 us (2%)
  between operations  16.2 us (1%)
    all_gather x1, blocking collectives, body(): lax.all_gather(router_weight, 'dp', axis=0, tiled=True)  156 us
    all_to_all x1, blocking collectives, to_experts(): return lax.all_to_all(joined, 'dp', split_axis=0, concat_axis=0, tiled=True)  144 us
    all_to_all x1, blocking collectives, from_experts(): lax.all_to_all(partial_rows, 'dp', split_axis=0, concat_axis=0, tiled=True)  142 us
    all_to_all x1, waiting for transfers between devices, to_experts(): return lax.all_to_all(joined, 'dp', split_axis=0, concat_axis=0, tiled=True)  138 us
    all_gather x2, waiting for transfers between devices, to_experts(): joined = lax.all_gather(buffer, 'tensor', axis=1, tiled=True)  89.4 us
    unnamed x2, blocking collectives  60.3 us
    dot_general x8, matrix products, bias_tile(): jnp.einsum('qkb,bh->hqk', onehot, bias_table, preferred_element_type=jnp....  45.7 us
    reduce_scatter x2, waiting for transfers between devices, from_experts(): lax.psum_scatter(returned.astype(jnp.float32).astype(jnp.bfloat16), 'tens...  40.4 us
  transfers between devices with their start and end apart: 12, of which 6 were waited for; matrix products, arithmetic and copies ran while one was open for 19% of the time, Pallas kernels for 0%

commit v1 on v0

v1 whole, which is shorter than its diff:
```python
import functools

import jax
import jax.numpy as jnp
from jax import lax
from jax.experimental import pallas as pl
from jax.experimental.pallas import tpu as pltpu
from jax.sharding import PartitionSpec as P

EPSILON = 1e-06
MASKED = -1e30
TILE = 256
F32 = jnp.float32
BF16 = jnp.bfloat16


def rms_scale(values):
    return lax.rsqrt(jnp.mean(values * values, axis=-1, keepdims=True) + EPSILON)


def dot_nn(a, b):
    return lax.dot_general(a, b, (((1,), (0,)), ((), ())), preferred_element_type=F32)


def dot_nt(a, b):
    return lax.dot_general(a, b, (((1,), (1,)), ((), ())), preferred_element_type=F32)


def dot_tn(a, b):
    return lax.dot_general(a, b, (((0,), (0,)), ((), ())), preferred_element_type=F32)


def tile_mask(segc_ref, segr_ref, start, keys):
    rows = start + lax.broadcasted_iota(jnp.int32, (TILE, keys), 0)
    cols = lax.broadcasted_iota(jnp.int32, (TILE, keys), 1)
    same = segc_ref[start : start + TILE, :] == segr_ref[:, :keys]
    return (cols <= rows) & same


def toeplitz(rv_row, length):
    return pltpu.roll(
        jnp.broadcast_to(rv_row, (TILE, length)), length - TILE + 1, 1, stride=1, stride_axis=0
    )


def attend_kernel(
    head_dim, x_ref, w_ref, rv_ref, segc_ref, segr_ref, part_ref, qkv_ref, o_ref, lse_ref, acc_ref
):
    head = pl.program_id(0)
    length = x_ref.shape[0]
    w = w_ref[0]
    qkv = dot_nn(x_ref[...], w[:, : 3 * head_dim]).astype(BF16)
    qkv_ref[0] = qkv
    scaled = qkv[:, :head_dim] * jnp.asarray(head_dim ** (-0.5), BF16)
    keys = qkv[:, head_dim : 2 * head_dim]
    vals = qkv[:, 2 * head_dim :]
    bias = toeplitz(rv_ref[0], length)
    for start in range(0, length, TILE):
        stop = start + TILE
        s = dot_nt(scaled[start:stop], keys[:stop]) + bias[:, length - stop :]
        s = jnp.where(tile_mask(segc_ref, segr_ref, start, stop), s, MASKED)
        top = jnp.max(s, axis=-1, keepdims=True)
        e = jnp.exp(s - top)
        total = jnp.sum(e, axis=-1, keepdims=True)
        p = (e * (1.0 / total)).astype(BF16)
        o_ref[0, start:stop, :] = dot_nn(p, vals[:stop]).astype(BF16)
        lse_ref[0, start:stop, :] = top + jnp.log(total)
    out_t = w[:, 3 * head_dim :]
    part = dot_nt(o_ref[0], out_t)

    @pl.when(head == 0)
    def _():
        acc_ref[...] = part

    @pl.when(head > 0)
    def _():
        acc_ref[...] += part

    @pl.when(head == pl.num_programs(0) - 1)
    def _():
        part_ref[...] = acc_ref[...].astype(BF16)


def attend_back_kernel(
    head_dim,
    x_ref,
    g_ref,
    w_ref,
    rv_ref,
    segc_ref,
    segr_ref,
    qkv_ref,
    o_ref,
    lse_ref,
    xin_ref,
    r1_ref,
    dx_ref,
    gw_ref,
    drv_ref,
    gfirst_ref,
    acc_ref,
    diag_ref,
    dqkv_ref,
):
    head = pl.program_id(0)
    length = x_ref.shape[0]
    w = w_ref[0]
    qkv = qkv_ref[0]
    factor = head_dim ** (-0.5)
    grad_o = dot_nn(g_ref[...], w[:, 3 * head_dim :]).astype(BF16)
    scaled = qkv[:, :head_dim] * jnp.asarray(factor, BF16)
    keys = qkv[:, head_dim : 2 * head_dim]
    vals = qkv[:, 2 * head_dim :]
    bias = toeplitz(rv_ref[0], length)
    dkv = [None] * (length // TILE)
    diag_ref[...] = jnp.zeros_like(diag_ref)
    for start in range(0, length, TILE):
        stop = start + TILE
        s = dot_nt(scaled[start:stop], keys[:stop]) + bias[:, length - stop :]
        s = jnp.where(tile_mask(segc_ref, segr_ref, start, stop), s, MASKED)
        p = jnp.exp(s - lse_ref[0, start:stop, :])
        do = grad_o[start:stop]
        dp = dot_nt(do, vals[:stop])
        delta = jnp.sum(p * dp, axis=-1, keepdims=True)
        ds = (p * (dp - delta)).astype(BF16)
        diag_ref[:, length - stop :] += ds.astype(F32)
        dqkv_ref[start:stop, :head_dim] = dot_nn(ds, keys[:stop]) * factor
        dk = dot_tn(ds, scaled[start:stop])
        dv = dot_tn(p.astype(BF16), do)
        both = jnp.concatenate([dk, dv], axis=1)
        if start == 0:
            dqkv_ref[:stop, head_dim:] = both
        else:
            dqkv_ref[:start, head_dim:] += both[:start]
            dqkv_ref[start:stop, head_dim:] = both[start:]
    x = diag_ref[...]
    half = TILE // 2
    while half >= 8:
        x = x[:half] + pltpu.roll(x[half : 2 * half], length - half, 1)
        half //= 2
    total = x[0:1]
    for row in range(1, 8):
        total = total + pltpu.roll(x[row : row + 1], length - row, 1)
    drv_ref[0] = pltpu.roll(total, TILE - 1, 1)
    dqkv = dqkv_ref[...].astype(BF16)
    gw_ref[0, :, : 3 * head_dim] = dot_tn(x_ref[...], dqkv).astype(gw_ref.dtype)
    gw_ref[0, :, 3 * head_dim :] = dot_tn(g_ref[...], o_ref[0]).astype(gw_ref.dtype)
    part = dot_nt(dqkv, w[:, : 3 * head_dim])

    @pl.when(head == 0)
    def _():
        acc_ref[...] = part

    @pl.when(head > 0)
    def _():
        acc_ref[...] += part

    @pl.when(head == pl.num_programs(0) - 1)
    def _():
        full = acc_ref[...]
        dx_ref[...] = full.astype(BF16)
        gfirst_ref[...] = jnp.sum(
            full * (xin_ref[...].astype(F32) * r1_ref[...]), axis=0, keepdims=True
        )


def whole(shape):
    return pl.BlockSpec(shape, lambda h: (0,) * len(shape))


def by_head(shape):
    return pl.BlockSpec((1,) + shape, lambda h: (h,) + (0,) * len(shape))


def attend(x, w, rv, segc, segr, head_dim):
    heads = w.shape[0]
    length, width = x.shape
    return pl.pallas_call(
        functools.partial(attend_kernel, head_dim),
        grid=(heads,),
        in_specs=[
            whole(x.shape),
            by_head(w.shape[1:]),
            by_head((1, length)),
            whole(segc.shape),
            whole(segr.shape),
        ],
        out_specs=[
            whole(x.shape),
            by_head((length, 3 * head_dim)),
            by_head((length, head_dim)),
            by_head((length, 1)),
        ],
        out_shape=[
            jax.ShapeDtypeStruct(x.shape, BF16),
            jax.ShapeDtypeStruct((heads, length, 3 * head_dim), BF16),
            jax.ShapeDtypeStruct((heads, length, head_dim), BF16),
            jax.ShapeDtypeStruct((heads, length, 1), F32),
        ],
        scratch_shapes=[pltpu.VMEM(x.shape, F32)],
        compiler_params=pltpu.CompilerParams(vmem_limit_bytes=40 * 2**20),
        cost_estimate=pl.CostEstimate(
            flops=15_000_000_000, bytes_accessed=8_000_000, transcendentals=2_000_000
        ),
    )(x, w, rv, segc, segr)


def attend_back(x, g, w, rv, segc, segr, qkv, o, lse, xin, r1, head_dim):
    heads = w.shape[0]
    length, width = x.shape
    return pl.pallas_call(
        functools.partial(attend_back_kernel, head_dim),
        grid=(heads,),
        in_specs=[
            whole(x.shape),
            whole(g.shape),
            by_head(w.shape[1:]),
            by_head((1, length)),
            whole(segc.shape),
            whole(segr.shape),
            by_head(qkv.shape[1:]),
            by_head(o.shape[1:]),
            by_head(lse.shape[1:]),
            whole(xin.shape),
            whole(r1.shape),
        ],
        out_specs=[
            whole(x.shape),
            by_head(w.shape[1:]),
            by_head((1, length)),
            whole((1, width)),
        ],
        out_shape=[
            jax.ShapeDtypeStruct(x.shape, BF16),
            jax.ShapeDtypeStruct(w.shape, BF16),
            jax.ShapeDtypeStruct((heads, 1, length), F32),
            jax.ShapeDtypeStruct((1, width), F32),
        ],
        scratch_shapes=[
            pltpu.VMEM(x.shape, F32),
            pltpu.VMEM((TILE, length), F32),
            pltpu.VMEM((length, 3 * head_dim), F32),
        ],
        compiler_params=pltpu.CompilerParams(vmem_limit_bytes=48 * 2**20),
        cost_estimate=pl.CostEstimate(
            flops=30_000_000_000, bytes_accessed=16_000_000, transcendentals=2_000_000
        ),
    )(x, g, w, rv, segc, segr, qkv, o, lse, xin, r1)


def swap_dp(rows):
    return lax.all_to_all(rows, "dp", split_axis=0, concat_axis=0, tiled=True)


def body(
    inputs,
    first_gain,
    qkv_weight,
    out_weight,
    bias_table,
    second_gain,
    router_weight,
    expert_in,
    expert_output_weights,
    segments,
    buckets,
    choices,
    cotangent,
):
    tokens_dev, model_width = inputs.shape
    n_dp = lax.axis_size("dp")
    n_tensor = lax.axis_size("tensor")
    rows_dp, heads_dev, triple = qkv_weight.shape
    head_dim = triple // 3
    experts = router_weight.shape[1]
    seq_len = segments.shape[1]
    bucket_count = bias_table.shape[0]
    top_count = choices.shape[1]
    capacity = max(2, 2 * top_count * tokens_dev // experts)
    slots = experts * capacity

    xin = lax.all_gather(inputs, "tensor", axis=0, tiled=True)
    packed = jnp.concatenate(
        [
            jnp.concatenate(
                [
                    qkv_weight,
                    jnp.transpose(out_weight).reshape(rows_dp, heads_dev, head_dim),
                ],
                axis=2,
            ).reshape(rows_dp, heads_dev * 4 * head_dim),
            first_gain[:, None],
            second_gain[:, None],
            router_weight,
        ],
        axis=1,
    )
    shared = lax.all_gather(packed, "dp", axis=0, tiled=True)
    wide = heads_dev * 4 * head_dim
    w_heads = jnp.transpose(
        shared[:, :wide].reshape(model_width, heads_dev, 4 * head_dim), (1, 0, 2)
    )
    first_f = shared[:, wide].astype(F32)
    second_f = shared[:, wide + 1].astype(F32)
    router_full = shared[:, wide + 2 :]

    ein, eout, xin = lax.optimization_barrier((expert_in, expert_output_weights, xin))
    w_in = lax.all_gather(ein, "tensor", axis=0, tiled=True)
    w_out = lax.all_gather(eout, "tensor", axis=0, tiled=True)

    onehot_bucket = buckets[:, None] == jnp.arange(bucket_count, dtype=jnp.int32)[None, :]
    by_gap = jnp.sum(
        jnp.where(onehot_bucket[:, None, :], jnp.transpose(bias_table)[None].astype(F32), 0.0),
        axis=2,
    )
    rv = jnp.transpose(by_gap[::-1])[:, None, :]

    xin_f = xin.astype(F32)
    r1_all = rms_scale(xin_f)
    xn1 = (xin_f * r1_all * first_f).astype(BF16)
    segc = segments.reshape(seq_len, 1)
    segr = segments.reshape(1, seq_len)
    part, qkv, mixed, lse = attend(xn1, w_heads, rv, segc, segr, head_dim)
    attn = lax.psum_scatter(part, "tensor", scatter_dimension=0, tiled=True).astype(F32)

    input_f = inputs.astype(F32)
    hidden = input_f + attn
    second_scale = rms_scale(hidden)
    normed_two = (hidden * second_scale * second_f).astype(BF16)
    logits = jnp.dot(normed_two, router_full, preferred_element_type=F32)
    probs = jax.nn.softmax(logits, axis=-1)

    pair_count = tokens_dev * top_count
    expert_range = jnp.arange(experts, dtype=jnp.int32)
    named = choices[:, :, None] == expert_range[None, None, :]
    named_flat = named.reshape(pair_count, experts)
    order = jnp.arange(pair_count, dtype=jnp.int32)
    earlier = (order[:, None] > order[None, :]).astype(BF16)
    before = jnp.dot(earlier, named_flat.astype(BF16), preferred_element_type=F32)
    slot = jnp.sum(jnp.where(named_flat, before, 0.0), axis=1).astype(jnp.int32)
    target = choices * capacity + slot.reshape(choices.shape)
    slot_range = jnp.arange(slots, dtype=jnp.int32)
    places = [(target[:, k : k + 1] == slot_range[None, :]).astype(BF16) for k in range(top_count)]

    picked = jnp.sum(jnp.where(named, probs[:, None, :], 0.0), axis=2)
    gate_sum = jnp.sum(picked, axis=1, keepdims=True)
    gates = picked / gate_sum
    grad_out = cotangent.astype(F32)

    send_rows = dot_tn(sum(places[1:], places[0]), normed_two).astype(BF16)
    grad_pairs = jnp.concatenate(
        [(gates[:, k : k + 1] * grad_out).astype(BF16) for k in range(top_count)], axis=0
    )
    send_grad = dot_tn(jnp.concatenate(places, axis=0), grad_pairs).astype(BF16)
    rows = swap_dp(send_rows.reshape(experts, capacity, model_width))
    grads = swap_dp(send_grad.reshape(experts, capacity, model_width))
    rows = rows.reshape(slots, model_width)
    grads = grads.reshape(slots, model_width)

    up = jnp.einsum("rd,qdf->qrf", rows, w_in, preferred_element_type=F32)
    active = jax.nn.gelu(up).astype(BF16)
    y = jnp.einsum("qrf,qfd->rd", active, w_out, preferred_element_type=F32).astype(BF16)
    y_back = swap_dp(y.reshape(experts, capacity, model_width)).reshape(slots, model_width)
    grad_active = jnp.einsum("rd,qfd->qrf", grads, w_out, preferred_element_type=F32)
    grad_up = jax.vjp(jax.nn.gelu, up)[1](grad_active)[0].astype(BF16)
    grad_rows = jnp.einsum("qrf,qdf->rd", grad_up, w_in, preferred_element_type=F32).astype(BF16)
    grad_back = swap_dp(grad_rows.reshape(experts, capacity, model_width))
    grad_back = grad_back.reshape(slots, model_width)
    part_out = jnp.einsum("qrf,rd->qfd", active, grads, preferred_element_type=F32).astype(BF16)
    part_in = jnp.einsum("rd,qrf->qdf", rows, grad_up, preferred_element_type=F32).astype(BF16)

    per_choice = [dot_nn(place, y_back) for place in places]
    result = hidden + sum(gates[:, k : k + 1] * per_choice[k] for k in range(top_count))
    grad_gate = jnp.concatenate(
        [jnp.sum(item * grad_out, axis=1, keepdims=True) for item in per_choice], axis=1
    )
    grad_picked = (grad_gate - jnp.sum(gates * grad_gate, axis=1, keepdims=True)) / gate_sum
    grad_probs = jnp.sum(jnp.where(named, grad_picked[:, :, None], 0.0), axis=1)
    grad_logits = (
        probs * (grad_probs - jnp.sum(probs * grad_probs, axis=1, keepdims=True))
    ).astype(BF16)
    grad_router = dot_tn(normed_two, grad_logits)
    grad_normed = dot_nt(grad_logits, router_full) + dot_nn(
        sum(places[1:], places[0]), grad_back
    )
    weighted = grad_normed * second_f
    scaled_hidden = hidden * second_scale
    grad_second = jnp.sum(grad_normed * scaled_hidden, axis=0)
    grad_hidden = (
        grad_out
        + second_scale * weighted
        - scaled_hidden
        * second_scale
        * second_scale
        * jnp.mean(weighted * hidden, axis=-1, keepdims=True)
    )
    grad_group = lax.all_gather(grad_hidden.astype(BF16), "tensor", axis=0, tiled=True)
    part_out, part_in, grad_group = lax.optimization_barrier((part_out, part_in, grad_group))
    grad_expert_out = lax.psum_scatter(
        part_out, "tensor", scatter_dimension=0, tiled=True
    ).astype(F32)
    grad_expert_in = lax.psum_scatter(part_in, "tensor", scatter_dimension=0, tiled=True).astype(
        F32
    )

    dx_part, gw_part, drv, grad_first = attend_back(
        xn1, grad_group, w_heads, rv, segc, segr, qkv, mixed, lse, xin, r1_all, head_dim
    )
    grad_first_in = lax.psum_scatter(dx_part, "tensor", scatter_dimension=0, tiled=True).astype(F32)
    first_scale = rms_scale(input_f)
    weighted_one = grad_first_in * first_f
    grad_inputs = (
        grad_hidden
        + first_scale * weighted_one
        - input_f
        * first_scale
        * first_scale
        * first_scale
        * jnp.mean(weighted_one * input_f, axis=-1, keepdims=True)
    )

    gw = lax.psum_scatter(
        jnp.transpose(gw_part, (1, 0, 2)), "dp", scatter_dimension=0, tiled=True
    ).astype(F32)
    grad_qkv_shard = gw[:, :, :triple]
    grad_out_shard = jnp.transpose(gw[:, :, triple:].reshape(rows_dp, heads_dev * head_dim))

    drv_gap = drv[:, 0, ::-1]
    table = jnp.sum(jnp.where(onehot_bucket[None], drv_gap[:, :, None], 0.0), axis=1)
    tensor_at = lax.axis_index("tensor")
    dp_at = lax.axis_index("dp")
    table_all = jnp.where(
        (jnp.arange(n_tensor) == tensor_at)[:, None, None], jnp.transpose(table)[None], 0.0
    )
    small = jnp.concatenate(
        [
            grad_first.reshape(-1),
            grad_second,
            grad_router.reshape(-1),
            table_all.reshape(-1),
        ]
    )
    small = lax.psum(small, ("dp", "tensor"))
    per_dev = model_width // (n_dp * n_tensor)
    own = (dp_at * n_tensor + tensor_at) * per_dev
    grad_first_shard = lax.dynamic_slice(small, (own,), (per_dev,))
    grad_second_shard = lax.dynamic_slice(small, (model_width + own,), (per_dev,))
    grad_router_shard = lax.dynamic_slice(
        small, (2 * model_width + own * experts,), (per_dev * experts,)
    ).reshape(per_dev, experts)
    table_size = bucket_count * heads_dev
    table_base = 2 * model_width + model_width * experts
    grad_table = lax.dynamic_slice(
        small, (table_base + tensor_at * table_size,), (table_size,)
    ).reshape(bucket_count, heads_dev)
    return (
        result,
        grad_inputs,
        grad_first_shard,
        grad_qkv_shard,
        grad_out_shard,
        grad_table,
        grad_second_shard,
        grad_router_shard,
        grad_expert_in,
        grad_expert_out,
    )


def solution(mesh):
    return jax.shard_map(
        body,
        mesh=mesh,
        in_specs=(
            P(("dp", "tensor"), None),
            P("dp"),
            P("dp", "tensor", None),
            P("tensor", "dp"),
            P(None, "tensor"),
            P("dp"),
            P("dp", None),
            P("dp", None, "tensor"),
            P("dp", "tensor", None),
            P("dp", None),
            P(),
            P(("dp", "tensor"), None),
            P(("dp", "tensor"), None),
        ),
        out_specs=(
            P(("dp", "tensor"), None),
            P(("dp", "tensor"), None),
            P(("dp", "tensor")),
            P("dp", "tensor", None),
            P("tensor", "dp"),
            P(None, "tensor"),
            P(("dp", "tensor")),
            P(("dp", "tensor"), None),
            P("dp", None, "tensor"),
            P("dp", "tensor", None),
        ),
        check_vma=False,
    )
```

time: 1290 us -> 629 us (0.49)
  blocking collectives: 591 us -> 121 us
  matrix products: 181 us -> 79.8 us
  local copies, waits for them, and re-layouts: 109 us -> 24.8 us
  Pallas kernels: 0 us -> 35.7 us
  loops' own time: 26.3 us -> 0 us
  other arithmetic: 41.6 us -> 23.3 us
    all_gather x3 -> x0, blocking collectives: 223 us -> none  [the longest x1 156 us: body(): lax.all_gather(router_weight, 'dp', axis=0, tiled=True)]
    all_to_all x2, blocking collectives: 286 us -> 83.8 us  [swap_dp(): return lax.all_to_all(rows, 'dp', split_axis=0, concat_axis=0, tiled=True)]
    reduce_scatter x5, waiting for transfers between devices: 63 us -> 164 us  [the longest x1 47.5 us: body(): lax.psum_scatter(part_in, 'tensor', scatter_dimension=0, tiled=True)]
    dot_general x35 -> x15, matrix products: 175 us -> 79.8 us  [the longest x1 14.6 us: body(): jnp.einsum('rd,qfd->qrf', grads, w_out, preferred_element_type=F32)]
    all_to_all x2, waiting for transfers between devices: 138 us -> 66.3 us  [swap_dp(): return lax.all_to_all(rows, 'dp', split_axis=0, concat_axis=0, tiled=True)]
    unnamed x2 -> x0, blocking collectives: 60.3 us -> none
    pallas_call x0 -> x2, Pallas kernels: none -> 35.7 us  [the longest x1 22.5 us: attend_back(): pl.pallas_call(functools.partial(attend_back_kernel, head_dim), grid=(hea...]
    all_gather x4 -> x5, waiting for transfers between devices: 109 us -> 77 us  [the longest x1 40.6 us: body(): shared = lax.all_gather(packed, 'dp', axis=0, tiled=True)]
  transfers between devices with their start and end apart: 12 -> 12, of which waited for: 6 -> 10; matrix products, arithmetic and copies ran while one was open for 19% -> 11% of each run, Pallas kernels for 0% -> 0%
where the time goes in v1:
time: 629 us; the launch traced here: 622 us
  waiting for transfers between devices  311 us (49%)
  blocking collectives  121 us (19%)
  matrix products  79.8 us (13%)
  Pallas kernels  35.7 us (6%)
  local copies, waits for them, and re-layouts  24.8 us (4%)
  other arithmetic  23.3 us (4%)
  between operations  15.4 us (2%)
  starting transfers between devices  10.7 us (2%)
    all_to_all x2, blocking collectives, swap_dp(): return lax.all_to_all(rows, 'dp', split_axis=0, concat_axis=0, tiled=True)  83.8 us
    all_to_all x2, waiting for transfers between devices, swap_dp(): return lax.all_to_all(rows, 'dp', split_axis=0, concat_axis=0, tiled=True)  66.3 us
    reduce_scatter x1, waiting for transfers between devices, body(): lax.psum_scatter(part_in, 'tensor', scatter_dimension=0, tiled=True)  47.5 us
    reduce_scatter x1, waiting for transfers between devices, body(): lax.psum_scatter(part_out, 'tensor', scatter_dimension=0, tiled=True)  46.1 us
    all_gather x1, waiting for transfers between devices, body(): shared = lax.all_gather(packed, 'dp', axis=0, tiled=True)  40.6 us
    psum x1, blocking collectives, body(): small = lax.psum(small, ('dp', 'tensor'))  37.4 us
    reduce_scatter x1, waiting for transfers between devices, body(): lax.psum_scatter(dx_part, 'tensor', scatter_dimension=0, tiled=True)  27.1 us
    reduce_scatter x1, waiting for transfers between devices, body(): lax.psum_scatter(part, 'tensor', scatter_dimension=0, tiled=True)  26.3 us
  transfers between devices with their start and end apart: 12, of which 10 were waited for; matrix products, arithmetic and copies ran while one was open for 11% of the time, Pallas kernels for 0%

profile of v1, /device:TPU:0, one launch (start us, length us, event | category | flops | bytes accessed | tf_op | source)
XLA Modules:
  0.0 621.7 jit_solution(9122323726971358842)
XLA Ops:
  7.2 0.9 copy.131
  8.1 1.0 maximum_bitcast_fusion
  9.2 0.8 copy.133
  9.9 0.8 copy.134
  10.7 0.8 copy.135
  11.5 0.8 pad_maximum_fusion
  12.3 0.7 all-gather.6.cloned.1.call-update
  13.8 0.7 iota_compare_fusion.6
  15.2 0.7 rev.6
  16.0 0.9 copy.138.segc_ref
  16.9 40.6 %all-gather.8.cloned.1.call-done = bf16[768,778]{1,0:T(8,128)(2,1)} async-done(((bf16[96,778]{1,0:T(8,128)(2,1)}), bf16[768,778]{1,0:T(8,128)(2,1)}) %all-gather.8.cloned.1.call-update) | async-done | bytes 1195024 | tf_op jit(solution)/shard_map/all_gather | solution.py:298
  57.4 1.3 slice.43
  60.1 1.3 convert_reduce_fusion
  61.4 15.8 %all-gather.6.cloned.1.call-done.xin_ref = bf16[1024,768]{1,0:T(8,128)(2,1)} async-done(((bf16[256,768]{1,0:T(8,128)(2,1)}), bf16[1024,768]{1,0:T(8,128)(2,1)}) %all-gather.6.cloned.1.call-update) | async-done | bytes 1572880 | tf_op jit(solution)/shard_map/all_gather | solution.py:282
  77.2 1.8 fusion.11
  79.1 1.8 fusion.13.x_ref
  80.9 13.2 %shard_map.204 = (bf16[1024,768]{1,0:T(8,128)(2,1)}, bf16[3,1024,192]{2,1,0:T(8,128)(2,1)S(1)}, bf16[3,1024,64]{2,1,0:T(8,128)(2,1)S(1)}, f32[3,1024,1]{2,1,0:T(8,128)S(1)}) custom-call(bf16[1024,768]{1,0:T(8,128)(2,1)S(1)} %fusion.13.x_ref, bf16[3,768,256]{2,1,0:T(8,128)(2,1)S(1)} %bitcast.93, f32[3,1,1024]{2,1,0:T(1,128)S(1)} %broadcast_in_dim.133.rv_ref, ...), custom_call_target="tpu_custom_call" | custom-call | flops 15000000512 | bytes 8000000 | tf_op jit(solution)/shard_map/pallas_call | solution.py:178
  94.1 1.2 copy-done.2
  95.3 1.1 copy-done.3
  96.4 0.9 copy-done.4
  99.4 26.3 %reduce-scatter.6.cloned.1.call-done = bf16[256,768]{1,0:T(8,128)(2,1)} async-done(((bf16[1024,768]{1,0:T(8,128)(2,1)}), bf16[256,768]{1,0:T(8,128)(2,1)}) %reduce-scatter.6.cloned.1.call-update) | async-done | bytes 393232 | tf_op jit(solution)/shard_map/reduce_scatter | solution.py:324
  125.7 1.2 multiply_reduce_fusion.2
  126.9 1.2 multiply_convert_fusion
  128.1 0.8 convolution_convert_fusion.2
  128.9 42.9 %all_to_all.20 = bf16[8,128,768]{2,1,0:T(8,128)(2,1)} all-to-all(bf16[8,128,768]{2,1,0:T(8,128)(2,1)S(1)} %bitcast.104), channel_id=1, replica_groups=mesh['dp'=8,'tensor'=4] {'dp'}, dimensions={0} | all-to-all | bytes 3145728 | tf_op jit(solution)/shard_map/all_to_all | solution.py:252
  171.9 11.2 %fusion.58 = f32[4,768,1024]{2,1,0:T(8,128)} fusion(bf16[4,768,768]{2,1,0:T(8,128)(2,1)} %all-gather.10.cloned.1.call-done, bf16[1024,768,1]{1,0,2:T(8,128)(2,1)} %bitcast.97), kind=kOutput, calls=%fused_computation.115 | convolution fusion | flops 4831838208 | bytes 18874368 | tf_op jit(solution)/shard_map/rd,qdf->qrf/dot_general | solution.py:360
  183.0 20.6 %all-gather.12.cloned.1.call-done = bf16[4,768,768]{2,1,0:T(8,128)(2,1)} async-done(((bf16[1,768,768]{2,1,0:T(8,128)(2,1)}), bf16[4,768,768]{2,1,0:T(8,128)(2,1)}) %all-gather.12.cloned.1.call-update) | async-done | bytes 4718608 | tf_op jit(solution)/shard_map/all_gather | solution.py:309
  203.7 11.3 %bitcast_convert_fusion.1 = bf16[1024,768]{1,0:T(8,128)(2,1)} fusion(bf16[4,768,768]{2,1,0:T(8,128)(2,1)} %all-gather.12.cloned.1.call-done, f32[4,768,1024]{2,1,0:T(8,128)} %fusion.58), kind=kOutput, calls=%fused_computation.23 | convolution fusion | flops 4860936192 | bytes 18874368 | tf_op jit(solution)/shard_map/qrf,qfd->rd/dot_general | solution.py:362
  215.0 5.6 all-to-all-start.1
  220.7 1.0 fusion.19
  221.7 1.3 fusion.57
  224.1 1.3 select_reduce_fusion.2
  225.4 32.7 %all-to-all-done.1 = bf16[8,128,768]{2,1,0:T(8,128)(2,1)} async-done(((bf16[8,128,768]{2,1,0:T(8,128)(2,1)}), bf16[8,128,768]{2,1,0:T(8,128)(2,1)}, u32[]{:S(2)}, u32[]{:S(2)}) %all-to-all-start.1) | async-done | bytes 1572896 | tf_op jit(solution)/shard_map/all_to_all | solution.py:252
  258.2 2.0 fusion.18
  260.2 0.9 copy-done.14
  261.1 2.9 fusion.28
  264.9 1.0 convolution_convert_fusion.1
  266.0 40.9 %all_to_all.21 = bf16[8,128,768]{2,1,0:T(8,128)(2,1)S(1)} all-to-all(bf16[8,128,768]{2,1,0:T(8,128)(2,1)S(1)} %bitcast.103), channel_id=1, replica_groups=mesh['dp'=8,'tensor'=4] {'dp'}, dimensions={0} | all-to-all | bytes 3145728 | tf_op jit(solution)/shard_map/all_to_all | solution.py:252
  306.9 14.6 %fusion.6 = bf16[4,1024,768]{1,2,0:T(8,128)(2,1)S(1)} fusion(f32[4,768,1024]{2,1,0:T(8,128)} %fusion.58, bf16[4,768,768]{2,1,0:T(8,128)(2,1)S(1)} %bitcast.133, bf16[1024,768,1]{1,0,2:T(8,128)(2,1)S(1)} %bitcast.99), kind=kOutput, calls=%fused_computation.8 | convolution fusion | flops 4894752768 | bytes 25165824 | tf_op jit(solution)/shard_map/rd,qfd->qrf/dot_general | solution.py:364
  321.6 6.3 %bitcast_convert_fusion = bf16[1024,768]{1,0:T(8,128)(2,1)} fusion(bf16[4,1024,768]{1,2,0:T(8,128)(2,1)S(1)} %fusion.6, bf16[4,768,768]{2,1,0:T(8,128)(2,1)S(1)} %bitcast.131), kind=kOutput, calls=%fused_computation.22 | convolution fusion | flops 4832624640 | bytes 12582912 | tf_op jit(solution)/shard_map/qrf,qdf->rd/dot_general | solution.py:366
  328.0 4.4 all-to-all-start.3
  332.9 2.2 fusion.38
  335.1 33.6 %all-to-all-done.3 = bf16[8,128,768]{2,1,0:T(8,128)(2,1)} async-done(((bf16[8,128,768]{2,1,0:T(8,128)(2,1)}), bf16[8,128,768]{2,1,0:T(8,128)(2,1)}, u32[]{:S(2)}, u32[]{:S(2)}) %all-to-all-start.3) | async-done | bytes 1572896 | tf_op jit(solution)/shard_map/all_to_all | solution.py:252
  368.7 3.3 multiply_reduce_fusion
  372.0 2.2 fusion.51
  374.5 9.0 %convert_bitcast_fusion = bf16[4,768,768]{1,2,0:T(8,128)(2,1)} fusion(bf16[4,1024,768]{1,2,0:T(8,128)(2,1)} %copy-done.53, bf16[1024,768,1]{1,0,2:T(8,128)(2,1)} %bitcast.98), kind=kOutput, calls=%fused_computation.16 | convolution fusion | flops 4834197504 | bytes 12582912 | tf_op jit(solution)/shard_map/rd,qrf->qdf/dot_general | solution.py:370
  383.5 12.4 %convolution_convert_fusion = bf16[4,768,768]{2,1,0:T(8,128)(2,1)} fusion(bf16[1024,768,1]{1,0,2:T(8,128)(2,1)} %bitcast.100, f32[4,768,1024]{2,1,0:T(8,128)} %fusion.58), kind=kOutput, calls=%fused_computation.24 | convolution fusion | flops 4862509056 | bytes 18874368 | tf_op jit(solution)/shard_map/qrf,rd->qfd/dot_general | solution.py:369
  395.9 22.5 %shard_map.205 = (bf16[1024,768]{1,0:T(8,128)(2,1)}, bf16[3,768,256]{2,1,0:T(8,128)(2,1)}, f32[3,1,1024]{2,1,0:T(1,128)S(1)}, f32[1,768]{1,0:T(1,128)S(1)}) custom-call(bf16[1024,768]{1,0:T(8,128)(2,1)} %copy-done, bf16[1024,768]{1,0:T(8,128)(2,1)} %all-gather.14.cloned.1.call-done.g_ref, bf16[3,768,256]{2,1,0:T(8,128)(2,1)S(1)} %bitcast.94, ...), custom_call_target="tpu_custom_call" | custom-call | flops 30000001024 | bytes 16000000 | tf_op jit(solution)/shard_map/pallas_call | solution.py:211
  418.5 0.7 reduce-scatter.8.cloned.1.call-update
  420.7 1.1 fusion.59
  421.7 1.2 reshape.246
  422.9 0.7 rev.7
  424.2 37.4 %psum.7 = f32[8064]{0:T(1024)S(1)} all-reduce(f32[8064]{0:T(1024)S(1)} %pad_maximum_fusion.1), channel_id=1, replica_groups=mesh['dp'=8,'tensor'=4] {'dp','tensor'}, use_global_device_ids=true, to_apply=%region_20.21 | all-reduce | flops 8064 | bytes 64512 | tf_op jit(solution)/shard_map/psum | solution.py:443
  463.9 16.7 %reduce-scatter.10.cloned.1.call-done = bf16[96,3,256]{2,0,1:T(8,128)(2,1)} async-done(((bf16[768,3,256]{2,0,1:T(8,128)(2,1)}), bf16[96,3,256]{2,0,1:T(8,128)(2,1)}) %reduce-scatter.10.cloned.1.call-update) | async-done | bytes 147472 | tf_op jit(solution)/shard_map/reduce_scatter | solution.py:422
  480.6 1.0 slice.51
  481.6 0.7 copy.148
  482.3 1.6 slice.50
  484.0 27.1 %reduce-scatter.8.cloned.1.call-done = bf16[256,768]{1,0:T(8,128)(2,1)} async-done(((bf16[1024,768]{1,0:T(8,128)(2,1)}), bf16[256,768]{1,0:T(8,128)(2,1)}) %reduce-scatter.8.cloned.1.call-update) | async-done | bytes 393232 | tf_op jit(solution)/shard_map/reduce_scatter | solution.py:409
  511.1 1.2 fusion.27
  512.4 3.1 fusion.26
  515.4 46.1 %reduce-scatter.14.cloned.1.call-done = bf16[1,768,768]{2,1,0:T(8,128)(2,1)} async-done(((bf16[4,768,768]{2,1,0:T(8,128)(2,1)}), bf16[1,768,768]{2,1,0:T(8,128)(2,1)}) %reduce-scatter.14.cloned.1.call-update) | async-done | bytes 1179664 | tf_op jit(solution)/shard_map/reduce_scatter | solution.py:399
  561.5 2.8 convert_element_type.143
  564.4 47.5 %reduce-scatter.12.cloned.1.call-done = bf16[1,768,768]{1,2,0:T(8,128)(2,1)} async-done(((bf16[4,768,768]{1,2,0:T(8,128)(2,1)}), bf16[1,768,768]{1,2,0:T(8,128)(2,1)}) %reduce-scatter.12.cloned.1.call-update) | async-done | bytes 1179664 | tf_op jit(solution)/shard_map/reduce_scatter | solution.py:402
  611.9 2.7 copy.151
  (178 shorter events, 11.7 us)
Async XLA Ops:
  7.2 50.3 %all-gather.8.cloned.1.call-start = ((), (), s32[]{:S(2)}) async-start(), calls=%async_computation.10 | async-start | bytes 1548288 | tf_op jit(solution)/shard_map/all_gather | solution.py:298
  12.3 65.0 %all-gather.6.cloned.1.call-start = ((), (), s32[]{:S(2)}) async-start(), calls=%async_computation.9 | async-start | bytes 1966080 | tf_op jit(solution)/shard_map/all_gather | solution.py:282
  13.0 112.6 %reduce-scatter.6.cloned.1.call-start = ((), (), s32[]{:S(2)}) async-start(), calls=%async_computation.11 | async-start | bytes 1966080 | tf_op jit(solution)/shard_map/reduce_scatter | solution.py:324
  58.8 22.1 %copy-start.1 = (s32[1,1024]{1,0:T(1,128)S(1)}, s32[1,1024]{1,0:T(1,128)}, u32[]{:S(2)}) copy-start(s32[1,1024]{1,0:T(1,128)} %segr_ref.3) | copy-start | bytes 12292
  61.4 32.7 %copy-start.25 = (f32[768]{0:T(1024)}, f32[768]{0:T(1024)S(1)}, u32[]{:S(2)}) copy-start(f32[768]{0:T(1024)S(1)} %get-tuple-element.101) | copy-start | bytes 9220
  61.4 65.5 %copy-start.23 = (f32[768]{0:T(1024)}, f32[768]{0:T(1024)S(1)}, u32[]{:S(2)}) copy-start(f32[768]{0:T(1024)S(1)} %get-tuple-element.100) | copy-start | bytes 9220
  79.0 15.0 %copy-start.27 = (f32[1024]{0:T(1024)}, f32[1024]{0:T(1024)S(1)}, u32[]{:S(2)}) copy-start(f32[1024]{0:T(1024)S(1)} %add_rsqrt_fusion) | copy-start | bytes 12292
  80.9 13.2 %copy-start = (bf16[1024,768]{1,0:T(8,128)(2,1)}, bf16[1024,768]{1,0:T(8,128)(2,1)S(1)}, u32[]{:S(2)}) copy-start(bf16[1024,768]{1,0:T(8,128)(2,1)S(1)} %fusion.13.x_ref) | copy-start | bytes 4718596
  80.9 17.6 %copy-start.29 = (s32[256,2]{0,1:T(2,128)S(1)}, s32[256,2]{0,1:T(2,128)}, u32[]{:S(2)}) copy-start(s32[256,2]{0,1:T(2,128)} %param.24) | copy-start | bytes 6148
  94.1 1.2 copy-start.2
  95.3 1.1 copy-start.3
  96.4 0.9 copy-start.4
  97.3 28.4 %copy-start.6 = (bf16[256,768]{1,0:T(8,128)(2,1)S(1)}, bf16[256,768]{1,0:T(8,128)(2,1)}, u32[]{:S(2)}) copy-start(bf16[256,768]{1,0:T(8,128)(2,1)} %param.13) | copy-start | bytes 1179652
  97.3 74.5 %all-gather.10.cloned.1.call-start = ((), (), s32[]{:S(2)}) async-start(), calls=%async_computation.12 | async-start | bytes 5898240 | tf_op jit(solution)/shard_map/all_gather | solution.py:308
  97.9 105.7 %all-gather.12.cloned.1.call-start = ((), (), s32[]{:S(2)}) async-start(), calls=%async_computation.13 | async-start | bytes 5898240 | tf_op jit(solution)/shard_map/all_gather | solution.py:309
  99.3 121.3 %copy-start.47 = (s32[256,1]{0,1:T(1,128)}, s32[256,1]{0,1:T(1,128)S(1)}, u32[]{:S(2)}) copy-start(s32[256,1]{0,1:T(1,128)S(1)} %get-tuple-element.118) | copy-start | bytes 3076
  99.3 121.3 %copy-start.51 = (s32[256,1]{0,1:T(1,128)}, s32[256,1]{0,1:T(1,128)S(1)}, u32[]{:S(2)}) copy-start(s32[256,1]{0,1:T(1,128)S(1)} %get-tuple-element.117) | copy-start | bytes 3076
  126.9 1.2 copy-start.35
  128.1 93.6 %copy-start.12 = (bf16[256,768]{1,0:T(8,128)(2,1)}, bf16[256,768]{1,0:T(8,128)(2,1)S(1)}, u32[]{:S(2)}) copy-start(bf16[256,768]{1,0:T(8,128)(2,1)S(1)} %multiply_convert_fusion) | copy-start | bytes 1179652
  215.0 46.1 %copy-start.8 = (bf16[256,768]{1,0:T(8,128)(2,1)S(1)}, bf16[256,768]{1,0:T(8,128)(2,1)}, u32[]{:S(2)}) copy-start(bf16[256,768]{1,0:T(8,128)(2,1)} %param.25) | copy-start | bytes 1179652
  215.0 43.2 %all-to-all-start.1 = ((bf16[8,128,768]{2,1,0:T(8,128)(2,1)}), bf16[8,128,768]{2,1,0:T(8,128)(2,1)}, u32[]{:S(2)}, u32[]{:S(2)}) async-start(bf16[8,128,768]{2,1,0:T(8,128)(2,1)} %bitcast.102), calls=%async_computation.2 | async-start | bytes 3145728 | tf_op jit(solution)/shard_map/all_to_all | solution.py:252
  223.0 41.9 %copy-start.18 = (bf16[256,1024]{1,0:T(8,128)(2,1)S(1)}, bf16[256,1024]{1,0:T(8,128)(2,1)}, u32[]{:S(2)}) copy-start(bf16[256,1024]{1,0:T(8,128)(2,1)} %get-tuple-element.124) | copy-start | bytes 1572868
  258.2 5.9 copy-start.45
  258.2 5.9 copy-start.49
  260.2 0.9 copy-start.14
  264.7 1.3 copy-start.37
  264.7 1.3 copy-start.39
  264.7 42.2 %slice-start.2 = ((s8[4718592]{0:T(1024)(128)(4,1)}), s8[4194304]{0:T(1024)(128)(4,1)S(1)}, s32[]{:S(2)}) async-start(s8[4718592]{0:T(1024)(128)(4,1)} %bitcast.132), calls=%async_computation.21 | async-start | bytes 8388608
  264.9 42.0 %slice-start.3 = ((s8[4718592]{0:T(1024)(128)(4,1)}), s8[524288]{0:T(1024)(128)(4,1)S(1)}, s32[]{:S(2)}) async-start(s8[4718592]{0:T(1024)(128)(4,1)} %bitcast.132), calls=%async_computation.22 | async-start | bytes 1048576
  266.0 55.5 %slice-start = ((s8[4718592]{0:T(1024)(128)(4,1)}), s8[524288]{0:T(1024)(128)(4,1)S(1)}, s32[]{:S(2)}) async-start(s8[4718592]{0:T(1024)(128)(4,1)} %bitcast.130), calls=%async_computation.19 | async-start | bytes 1048576
  306.9 14.6 %copy-start.17 = (bf16[8,128,768]{2,1,0:T(8,128)(2,1)}, bf16[8,128,768]{2,1,0:T(8,128)(2,1)S(1)}, u32[]{:S(2)}) copy-start(bf16[8,128,768]{2,1,0:T(8,128)(2,1)S(1)} %all_to_all.21) | copy-start | bytes 4718596
  306.9 14.6 %slice-start.1 = ((s8[4718592]{0:T(1024)(128)(4,1)}), s8[4194304]{0:T(1024)(128)(4,1)S(1)}, s32[]{:S(2)}) async-start(s8[4718592]{0:T(1024)(128)(4,1)} %bitcast.130), calls=%async_computation.20 | async-start | bytes 8388608
  321.5 6.4 %copy-start.53 = (bf16[4,1024,768]{1,2,0:T(8,128)(2,1)}, bf16[4,1024,768]{1,2,0:T(8,128)(2,1)S(1)}, u32[]{:S(2)}) copy-start(bf16[4,1024,768]{1,2,0:T(8,128)(2,1)S(1)} %fusion.6) | copy-start | bytes 18874372
  321.5 10.9 %copy-start.28 = (f32[1024]{0:T(1024)S(1)}, f32[1024]{0:T(1024)}, u32[]{:S(2)}) copy-start(f32[1024]{0:T(1024)} %copy-done.27) | copy-start | bytes 12292
  321.5 11.2 %copy-start.42 = (f32[256]{0:T(256)S(1)}, f32[256]{0:T(256)}, u32[]{:S(2)}) copy-start(f32[256]{0:T(256)} %copy-done.41) | copy-start | bytes 3076
  321.6 11.2 %copy-start.44 = (f32[256]{0:T(256)S(1)}, f32[256]{0:T(256)}, u32[]{:S(2)}) copy-start(f32[256]{0:T(256)} %copy-done.43) | copy-start | bytes 3076
  321.6 11.2 %copy-start.46 = (f32[256]{0:T(256)S(1)}, f32[256]{0:T(256)}, u32[]{:S(2)}) copy-start(f32[256]{0:T(256)} %get-tuple-element.105) | copy-start | bytes 3076
  321.6 11.2 %copy-start.50 = (f32[256]{0:T(256)S(1)}, f32[256]{0:T(256)}, u32[]{:S(2)}) copy-start(f32[256]{0:T(256)} %get-tuple-element.107) | copy-start | bytes 3076
  321.6 11.2 %copy-start.30 = (s32[256,2]{0,1:T(2,128)S(1)}, s32[256,2]{0,1:T(2,128)}, u32[]{:S(2)}) copy-start(s32[256,2]{0,1:T(2,128)} %param.24) | copy-start | bytes 6148
  321.6 11.2 %copy-start.22 = (f32[256,8]{0,1:T(8,128)S(1)}, f32[256,8]{0,1:T(8,128)}, u32[]{:S(2)}) copy-start(f32[256,8]{0,1:T(8,128)} %copy-done.21) | copy-start | bytes 24580
  321.6 11.2 %copy-start.32 = (f32[256]{0:T(256)S(1)}, f32[256]{0:T(256)}, u32[]{:S(2)}) copy-start(f32[256]{0:T(256)} %copy-done.31) | copy-start | bytes 3076
  321.6 11.2 %copy-start.34 = (f32[256]{0:T(256)S(1)}, f32[256]{0:T(256)}, u32[]{:S(2)}) copy-start(f32[256]{0:T(256)} %copy-done.33) | copy-start | bytes 3076
  328.0 40.7 %copy-start.10 = (bf16[256,768]{1,0:T(8,128)(2,1)S(1)}, bf16[256,768]{1,0:T(8,128)(2,1)}, u32[]{:S(2)}) copy-start(bf16[256,768]{1,0:T(8,128)(2,1)} %reduce-scatter.6.cloned.1.call-done) | copy-start | bytes 1179652
  328.0 40.7 %copy-start.24 = (f32[768]{0:T(1024)S(1)}, f32[768]{0:T(1024)}, u32[]{:S(2)}) copy-start(f32[768]{0:T(1024)} %copy-done.23) | copy-start | bytes 9220
  328.0 40.7 %copy-start.36 = (f32[256]{0:T(256)S(1)}, f32[256]{0:T(256)}, u32[]{:S(2)}) copy-start(f32[256]{0:T(256)} %copy-done.35) | copy-start | bytes 3076
  328.0 40.7 %copy-start.48 = (s32[256,1]{0,1:T(1,128)S(1)}, s32[256,1]{0,1:T(1,128)}, u32[]{:S(2)}) copy-start(s32[256,1]{0,1:T(1,128)} %copy-done.47) | copy-start | bytes 3076
  328.0 40.7 %copy-start.52 = (s32[256,1]{0,1:T(1,128)S(1)}, s32[256,1]{0,1:T(1,128)}, u32[]{:S(2)}) copy-start(s32[256,1]{0,1:T(1,128)} %copy-done.51) | copy-start | bytes 3076
  328.0 40.7 %all-to-all-start.3 = ((bf16[8,128,768]{2,1,0:T(8,128)(2,1)}), bf16[8,128,768]{2,1,0:T(8,128)(2,1)}, u32[]{:S(2)}, u32[]{:S(2)}) async-start(bf16[8,128,768]{2,1,0:T(8,128)(2,1)} %bitcast.101), calls=%async_computation.4 | async-start | bytes 3145728 | tf_op jit(solution)/shard_map/all_to_all | solution.py:252
  332.4 63.5 %all-gather.14.cloned.1.call-start = ((), (), s32[]{:S(2)}) async-start(), calls=%async_computation.14 | async-start | bytes 1966080 | tf_op jit(solution)/shard_map/all_gather | solution.py:397
  374.2 106.4 %reduce-scatter.10.cloned.1.call-start = ((), (), s32[]{:S(2)}) async-start(), calls=%async_computation.16 | async-start | bytes 1327104 | tf_op jit(solution)/shard_map/reduce_scatter | solution.py:422
  383.5 12.4 %copy-start.5 = (bf16[3,1024,64]{2,1,0:T(8,128)(2,1)S(1)}, bf16[3,1024,64]{2,1,0:T(8,128)(2,1)}, u32[]{:S(2)}) copy-start(bf16[3,1024,64]{2,1,0:T(8,128)(2,1)} %copy-done.4) | copy-start | bytes 1179652
  418.5 92.6 %reduce-scatter.8.cloned.1.call-start = ((), (), s32[]{:S(2)}) async-start(), calls=%async_computation.15 | async-start | bytes 1966080 | tf_op jit(solution)/shard_map/reduce_scatter | solution.py:409
  419.2 1.5 copy-start.13
  419.2 4.5 copy-start.20
  419.2 142.3 %reduce-scatter.14.cloned.1.call-start = ((), (), s32[]{:S(2)}) async-start(), calls=%async_computation.18 | async-start | bytes 5898240 | tf_op jit(solution)/shard_map/reduce_scatter | solution.py:399
  420.0 91.1 %copy-start.7 = (bf16[256,768]{1,0:T(8,128)(2,1)S(1)}, bf16[256,768]{1,0:T(8,128)(2,1)}, u32[]{:S(2)}) copy-start(bf16[256,768]{1,0:T(8,128)(2,1)} %param.13) | copy-start | bytes 1179652
  420.0 91.1 %copy-start.26 = (f32[768]{0:T(1024)S(1)}, f32[768]{0:T(1024)}, u32[]{:S(2)}) copy-start(f32[768]{0:T(1024)} %copy-done.25) | copy-start | bytes 9220
  420.0 92.3 %copy-start.9 = (bf16[256,768]{1,0:T(8,128)(2,1)S(1)}, bf16[256,768]{1,0:T(8,128)(2,1)}, u32[]{:S(2)}) copy-start(bf16[256,768]{1,0:T(8,128)(2,1)} %param.25) | copy-start | bytes 1179652
  420.0 92.3 %copy-start.11 = (bf16[256,768]{1,0:T(8,128)(2,1)S(1)}, bf16[256,768]{1,0:T(8,128)(2,1)}, u32[]{:S(2)}) copy-start(bf16[256,768]{1,0:T(8,128)(2,1)} %reduce-scatter.6.cloned.1.call-done) | copy-start | bytes 1179652
  420.0 92.3 %copy-start.15 = (f32[256,768]{1,0:T(8,128)S(1)}, f32[256,768]{1,0:T(8,128)}, u32[]{:S(2)}) copy-start(f32[256,768]{1,0:T(8,128)} %copy-done.14) | copy-start | bytes 2359300
  420.0 92.3 %copy-start.16 = (f32[256,768]{1,0:T(8,128)S(1)}, f32[256,768]{1,0:T(8,128)}, u32[]{:S(2)}) copy-start(f32[256,768]{1,0:T(8,128)} %get-tuple-element.119) | copy-start | bytes 2359300
  420.0 92.3 %copy-start.38 = (f32[256,1]{0,1:T(1,128)S(1)}, f32[256,1]{0,1:T(1,128)}, u32[]{:S(2)}) copy-start(f32[256,1]{0,1:T(1,128)} %copy-done.37) | copy-start | bytes 3076
  420.0 92.3 %copy-start.40 = (f32[256,1]{0,1:T(1,128)S(1)}, f32[256,1]{0,1:T(1,128)}, u32[]{:S(2)}) copy-start(f32[256,1]{0,1:T(1,128)} %copy-done.39) | copy-start | bytes 3076
  420.1 191.8 %reduce-scatter.12.cloned.1.call-start = ((), (), s32[]{:S(2)}) async-start(), calls=%async_computation.17 | async-start | bytes 5898240 | tf_op jit(solution)/shard_map/reduce_scatter | solution.py:402
  (6 other events, 4.1 us)
Sparse Core Ops, SparseCore 0:
  12.4 44.9 all-gather.7
  59.0 18.2 all-gather.5
  97.5 28.1 reduce-scatter.5
  127.2 37.4 all-gather.9
  166.2 37.4 all-gather.11
  374.3 17.6 all-gather.13
  418.6 61.9 reduce-scatter.9
  483.9 27.1 reduce-scatter.7
  513.6 47.8 reduce-scatter.13
  564.1 47.7 reduce-scatter.11
